TPU v7x, 128 devices: a whole 4x4x4 slice. The times are simulated.
128 devices in a mesh: ctx: 16 (over z, y_lo, core), head: 8 (over x, y_hi).
Axes of the slice: x: 4, y: 4 (y_hi: 2, y_lo: 2; y = y_hi * 2 + y_lo), z: 4, core: 2. Of those that a mesh axis runs over, the one named last changes fastest.
Arguments:
- tokens: bfloat16 [3072, 2048], P('ctx', 'head'), may hold values from -6 to 6
- norm_gain: float32 [2048], replicated, may hold values from 0.25 to 1.75
- w_query: bfloat16 [2048, 2048], P(None, 'head'), may hold values from -0.125 to 0.125
- w_key: bfloat16 [2048, 2048], P(None, 'head'), may hold values from -0.125 to 0.125
- w_value: bfloat16 [2048, 2048], P(None, 'head'), may hold values from -0.125 to 0.125
- w_out: bfloat16 [2048, 2048], P('head'), may hold values from -0.125 to 0.125
- teacher: bfloat16 [3, 3072, 2048], P(None, 'ctx', 'head'), may hold values from -6 to 6
Outputs:
- grad_input: float32 [3072, 2048], P('ctx', 'head')
- grad_gain: float32 [2048], replicated
- grad_query: float32 [2048, 2048], P('ctx', 'head')
- grad_key: float32 [2048, 2048], P('ctx', 'head')
- grad_value: float32 [2048, 2048], P('ctx', 'head')
- grad_outproj: float32 [2048, 2048], P('head', 'ctx')
All inputs are finite; a program needn't handle non-finite values.
Results may differ from a plain program's by a relative error of at most 0.015.
Values may be sent and summed in bfloat16 or wider, within the bound.
No kernel may reach another device: no remote copies, remote signals or barrier semaphores. Data moves between devices by JAX's collectives and lax.ppermute only.
A program may use at most 128 MiB of HBM per device.

v0:
```python
import math

import jax
import jax.numpy as jnp
from jax import lax
from jax.sharding import PartitionSpec as P

DH = 128
RECUR = 3


EPSILON = 1e-06
MASKED = -1e30


def normalize(state, norm_gain):
    inverse = lax.rsqrt(jnp.mean(state * state, axis=-1, keepdims=True) + EPSILON)
    scaled = state * inverse
    return ((scaled * norm_gain).astype(jnp.bfloat16), scaled, inverse)


def split_heads(block):
    return jnp.transpose(block.reshape(block.shape[0], -1, DH), (1, 0, 2))


def join_heads(block):
    return jnp.transpose(block, (1, 0, 2)).reshape(block.shape[1], -1)


def masked_scores(query, key_block, query_pos, key_pos):
    scaling = 1.0 / math.sqrt(query.shape[-1])
    scores = jnp.dot(query, key_block.T, preferred_element_type=jnp.float32) * scaling
    return jnp.where(key_pos[None, :] <= query_pos[:, None], scores, MASKED)


def attend(query, key_block, value_block, query_pos, key_pos):
    scores = masked_scores(query, key_block, query_pos, key_pos)
    row_max = jnp.max(scores, axis=-1, keepdims=True)
    weights = jnp.exp(scores - row_max)
    denominator = jnp.sum(weights, axis=-1, keepdims=True)
    probabilities = (weights / denominator).astype(jnp.bfloat16)
    attended = jnp.dot(probabilities, value_block, preferred_element_type=jnp.float32).astype(
        jnp.bfloat16
    )
    return (attended, row_max[:, 0] + jnp.log(denominator[:, 0]))


def score_grads(
    query, key_block, value_block, grad_attended, row_dot, log_total, query_pos, key_pos
):
    scores = masked_scores(query, key_block, query_pos, key_pos)
    probabilities = jnp.exp(scores - log_total[:, None])
    grad_probs = jnp.dot(grad_attended, value_block.T, preferred_element_type=jnp.float32)
    grad_scores = (probabilities * (grad_probs - row_dot[:, None])).astype(jnp.bfloat16)
    return (probabilities.astype(jnp.bfloat16), grad_scores)


def both_grads(
    query, key_block, value_block, grad_attended, row_dot, log_total, query_pos, key_pos
):
    scaling = 1.0 / math.sqrt(query.shape[-1])
    rounded, grad_scores = score_grads(
        query, key_block, value_block, grad_attended, row_dot, log_total, query_pos, key_pos
    )
    grad_rows = (
        jnp.dot(grad_scores, key_block, preferred_element_type=jnp.float32) * scaling
    ).astype(jnp.bfloat16)
    key_term = jnp.dot(grad_scores.T, query, preferred_element_type=jnp.float32) * scaling
    value_term = jnp.dot(rounded.T, grad_attended, preferred_element_type=jnp.float32)
    return (grad_rows, key_term, value_term)


def body(tokens, norm_gain, w_query, w_key, w_value, w_out, teacher):
    local_rows = tokens.shape[0]
    shards = lax.axis_size("ctx")
    offset = lax.axis_index("ctx") * local_rows
    query_pos = offset + jnp.arange(local_rows, dtype=jnp.int32)
    key_pos = jnp.arange(local_rows * shards, dtype=jnp.int32)
    head_map = (0, 0, 0, None, None)
    grad_map = (0, 0, 0, 0, 0, 0, None, None)
    state = tokens.astype(jnp.float32)
    states = [state]
    normed_list = []
    scaled_list = []
    inverses = []
    queries = []
    attended_list = []
    totals = []
    for level in range(RECUR):
        gathered = lax.all_gather(state, "head", axis=1, tiled=True)
        normed, scaled, inverse = normalize(gathered, norm_gain)
        query_rows = jnp.dot(normed, w_query, preferred_element_type=jnp.float32).astype(
            jnp.bfloat16
        )
        if level == 0:
            own_keys = jnp.dot(normed, w_key, preferred_element_type=jnp.float32).astype(
                jnp.bfloat16
            )
            own_values = jnp.dot(normed, w_value, preferred_element_type=jnp.float32).astype(
                jnp.bfloat16
            )
            keys_whole, values_whole = (
                lax.all_gather(own_keys, "ctx", axis=0, tiled=True),
                lax.all_gather(own_values, "ctx", axis=0, tiled=True),
            )
            key_heads = split_heads(keys_whole)
            value_heads = split_heads(values_whole)
        attended_heads, log_total = jax.vmap(attend, in_axes=head_map)(
            split_heads(query_rows), key_heads, value_heads, query_pos, key_pos
        )
        attended = join_heads(attended_heads)
        partial_value = jnp.dot(attended, w_out, preferred_element_type=jnp.float32)
        state = state + lax.psum_scatter(partial_value, "head", scatter_dimension=1, tiled=True)
        states.append(state)
        normed_list.append(normed)
        scaled_list.append(scaled)
        inverses.append(inverse)
        queries.append(query_rows)
        attended_list.append(attended)
        totals.append(log_total)
    weight = 1.0 / math.sqrt(local_rows * shards)
    model_width = w_query.shape[0]
    head_width = w_query.shape[1]
    heads_local = head_width // DH
    grad = jnp.zeros_like(state)
    grad_query = jnp.zeros((model_width, head_width), jnp.float32)
    grad_outproj = jnp.zeros((head_width, model_width), jnp.float32)
    grad_gain = jnp.zeros((model_width,), jnp.float32)
    key_sum = jnp.zeros((heads_local, local_rows * shards, DH), jnp.float32)
    value_sum = jnp.zeros((heads_local, local_rows * shards, DH), jnp.float32)
    for level in range(RECUR - 1, -1, -1):
        grad = grad + weight * (states[level + 1] - teacher[level].astype(jnp.float32))
        grad_round = grad.astype(jnp.bfloat16)
        grad_whole = lax.all_gather(grad_round, "head", axis=1, tiled=True)
        grad_outproj = grad_outproj + jnp.dot(
            attended_list[level].T, grad_whole, preferred_element_type=jnp.float32
        )
        grad_attended = jnp.dot(grad_whole, w_out.T, preferred_element_type=jnp.float32).astype(
            jnp.bfloat16
        )
        grad_heads = split_heads(grad_attended)
        row_dot = jnp.sum(
            grad_heads.astype(jnp.float32) * split_heads(attended_list[level]).astype(jnp.float32),
            axis=-1,
        )
        query_heads = split_heads(queries[level])
        grad_query_heads, key_term, value_term = jax.vmap(both_grads, in_axes=grad_map)(
            query_heads,
            key_heads,
            value_heads,
            grad_heads,
            row_dot,
            totals[level],
            query_pos,
            key_pos,
        )
        key_sum = key_sum + key_term
        value_sum = value_sum + value_term
        grad_query_rows = join_heads(grad_query_heads)
        grad_normed = jnp.dot(grad_query_rows, w_query.T, preferred_element_type=jnp.float32)
        grad_query = grad_query + jnp.dot(
            normed_list[level].T, grad_query_rows, preferred_element_type=jnp.float32
        )
        if level == 0:
            key_own, value_own = (
                lax.psum_scatter(join_heads(key_sum), "ctx", scatter_dimension=0, tiled=True),
                lax.psum_scatter(join_heads(value_sum), "ctx", scatter_dimension=0, tiled=True),
            )
            grad_keys = key_own.astype(jnp.bfloat16)
            grad_values = value_own.astype(jnp.bfloat16)
            grad_normed = grad_normed + jnp.dot(
                grad_keys, w_key.T, preferred_element_type=jnp.float32
            )
            grad_normed = grad_normed + jnp.dot(
                grad_values, w_value.T, preferred_element_type=jnp.float32
            )
            grad_key = jnp.dot(normed_list[0].T, grad_keys, preferred_element_type=jnp.float32)
            grad_value = jnp.dot(normed_list[0].T, grad_values, preferred_element_type=jnp.float32)
        scaled = scaled_list[level]
        grad_gain = grad_gain + jnp.sum(grad_normed * scaled, axis=0)
        back = grad_normed * norm_gain
        partial_value = inverses[level] * (
            back - scaled * jnp.mean(back * scaled, axis=-1, keepdims=True)
        )
        grad = grad + lax.psum_scatter(partial_value, "head", scatter_dimension=1, tiled=True)
    stacked = jnp.stack([grad_query, grad_key, grad_value, grad_outproj.T])
    summed = lax.psum_scatter(stacked, "ctx", scatter_dimension=1, tiled=True)
    grad_gain = lax.psum(grad_gain, ("ctx", "head"))
    return (grad, grad_gain, summed[0], summed[1], summed[2], summed[3].T)


def solution(mesh):
    return jax.shard_map(
        body,
        mesh=mesh,
        in_specs=(
            P("ctx", "head"),
            P(),
            P(None, "head"),
            P(None, "head"),
            P(None, "head"),
            P("head", None),
            P(None, "ctx", "head"),
        ),
        out_specs=(
            P("ctx", "head"),
            P(),
            P("ctx", "head"),
            P("ctx", "head"),
            P("ctx", "head"),
            P("head", "ctx"),
        ),
        check_vma=False,
    )
```

profile of v0, /device:TPU:0, one launch (start us, length us, event | category | flops | bytes accessed | tf_op | source)
XLA Modules:
  0.0 1104.6 jit_solution(9262222009377230296)
XLA Ops:
  9.0 56.9 %all-gather.6.cloned.1.call-done = f32[192,2048]{1,0:T(8,128)} async-done(((f32[192,256]{1,0:T(8,128)}), f32[192,2048]{1,0:T(8,128)}) %all-gather.6.cloned.1.call-update) | async-done | bytes 1572880 | tf_op jit(solution)/shard_map/all_gather | solution.py:90
  71.8 30.3 %all-gather.8.cloned.1.call-done = bf16[3072,256]{1,0:T(8,128)(2,1)} async-done(((bf16[192,256]{1,0:T(8,128)(2,1)}), bf16[3072,256]{1,0:T(8,128)(2,1)}) %all-gather.8.cloned.1.call-update) | async-done | bytes 1572880 | tf_op jit(solution)/shard_map/all_gather | solution.py:103
  104.7 2.7 fusion.111
  110.4 27.4 %all-gather.10.cloned.1.call-done = bf16[3072,256]{1,0:T(8,128)(2,1)} async-done(((bf16[192,256]{1,0:T(8,128)(2,1)}), bf16[3072,256]{1,0:T(8,128)(2,1)}) %all-gather.10.cloned.1.call-update) | async-done | bytes 1572880 | tf_op jit(solution)/shard_map/all_gather | solution.py:104
  137.8 3.9 fusion.42
  143.4 74.3 %reduce-scatter.14.cloned.1.call-done = f32[192,256]{1,0:T(8,128)} async-done(((f32[192,2048]{1,0:T(8,128)}), f32[192,256]{1,0:T(8,128)}) %reduce-scatter.14.cloned.1.call-update) | async-done | bytes 196624 | tf_op jit(solution)/shard_map/reduce_scatter | solution.py:113
  219.4 52.5 %all-gather.12.cloned.1.call-done = f32[192,2048]{1,0:T(8,128)} async-done(((f32[192,256]{1,0:T(8,128)}), f32[192,2048]{1,0:T(8,128)}) %all-gather.12.cloned.1.call-update) | async-done | bytes 1572880 | tf_op jit(solution)/shard_map/all_gather | solution.py:90
  281.3 73.1 %reduce-scatter.16.cloned.1.call-done = f32[192,256]{1,0:T(8,128)} async-done(((f32[192,2048]{1,0:T(8,128)}), f32[192,256]{1,0:T(8,128)}) %reduce-scatter.16.cloned.1.call-update) | async-done | bytes 196624 | tf_op jit(solution)/shard_map/reduce_scatter | solution.py:113
  356.6 51.5 %all-gather.14.cloned.1.call-done = f32[192,2048]{1,0:T(8,128)} async-done(((f32[192,256]{1,0:T(8,128)}), f32[192,2048]{1,0:T(8,128)}) %all-gather.14.cloned.1.call-update) | async-done | bytes 1572880 | tf_op jit(solution)/shard_map/all_gather | solution.py:90
  417.5 2.6 copy.221
  420.1 70.5 %reduce-scatter.18.cloned.1.call-done = f32[192,256]{1,0:T(8,128)} async-done(((f32[192,2048]{1,0:T(8,128)}), f32[192,256]{1,0:T(8,128)}) %reduce-scatter.18.cloned.1.call-update) | async-done | bytes 196624 | tf_op jit(solution)/shard_map/reduce_scatter | solution.py:113
  491.9 35.7 %all_gather.29 = bf16[192,2048]{1,0:T(8,128)(2,1)S(1)} all-gather(bf16[192,256]{1,0:T(8,128)(2,1)S(1)} %fusion.57), channel_id=1, replica_groups=mesh['ctx'=16,'head'=8] {'head'}, dimensions={1}, use_global_device_ids=true | all-gather | bytes 884736 | tf_op jit(solution)/shard_map/all_gather | solution.py:134
  530.7 3.7 multiply_convert_fusion.2
  539.0 73.3 %reduce-scatter.20.cloned.1.call-done = f32[192,256]{1,0:T(8,128)} async-done(((f32[192,2048]{1,0:T(8,128)}), f32[192,256]{1,0:T(8,128)}) %reduce-scatter.20.cloned.1.call-update) | async-done | bytes 196624 | tf_op jit(solution)/shard_map/reduce_scatter | solution.py:185
  614.4 35.7 %all_gather.30 = bf16[192,2048]{1,0:T(8,128)(2,1)S(1)} all-gather(bf16[192,256]{1,0:T(8,128)(2,1)S(1)} %get-tuple-element.32), channel_id=1, replica_groups=mesh['ctx'=16,'head'=8] {'head'}, dimensions={1}, use_global_device_ids=true | all-gather | bytes 884736 | tf_op jit(solution)/shard_map/all_gather | solution.py:134
  651.2 3.7 multiply_convert_fusion.1
  664.1 68.4 %reduce-scatter.22.cloned.1.call-done = f32[192,256]{1,0:T(8,128)} async-done(((f32[192,2048]{1,0:T(8,128)}), f32[192,256]{1,0:T(8,128)}) %reduce-scatter.22.cloned.1.call-update) | async-done | bytes 196624 | tf_op jit(solution)/shard_map/reduce_scatter | solution.py:185
  734.4 35.7 %all_gather.31 = bf16[192,2048]{1,0:T(8,128)(2,1)S(1)} all-gather(bf16[192,256]{1,0:T(8,128)(2,1)S(1)} %get-tuple-element.30), channel_id=1, replica_groups=mesh['ctx'=16,'head'=8] {'head'}, dimensions={1}, use_global_device_ids=true | all-gather | bytes 884736 | tf_op jit(solution)/shard_map/all_gather | solution.py:134
  772.4 3.7 multiply_convert_fusion
  778.5 3.5 copy.55
  782.1 3.5 fusion.11
  785.7 3.6 convolution_add_fusion.1
  789.4 3.0 convolution_add_fusion
  792.3 3.5 copy.57
  796.0 2.9 fusion.51
  800.7 47.5 %reduce-scatter.28.cloned.1.call-done = f32[192,256]{1,0:T(8,128)} async-done(((f32[3072,256]{1,0:T(8,128)}), f32[192,256]{1,0:T(8,128)}) %reduce-scatter.28.cloned.1.call-update) | async-done | bytes 196624
  849.2 3.5 convolution_add_fusion.9
  852.7 63.2 %reduce-scatter.30.cloned.1.call-done = f32[192,256]{1,0:T(8,128)} async-done(((f32[3072,256]{1,0:T(8,128)}), f32[192,256]{1,0:T(8,128)}) %reduce-scatter.30.cloned.1.call-update) | async-done | bytes 196624
  917.7 3.9 multiply_reduce_fusion
  931.1 3.6 pad_maximum_fusion
  935.4 66.9 %psum.7 = f32[2048]{0:T(1024)} all-reduce(f32[2048]{0:T(1024)S(1)} %add_add_fusion), channel_id=1, replica_groups=mesh['ctx'=16,'head'=8] {'ctx','head'}, use_global_device_ids=true, to_apply=%region_26.27 | all-reduce | flops 2048 | bytes 16384 | tf_op jit(solution)/shard_map/psum | solution.py:188
  1004.0 91.2 %reduce-scatter.26.cloned.1.call-done = f32[4,128,256]{2,1,0:T(8,128)} async-done(((f32[4,2048,256]{2,1,0:T(8,128)}), f32[4,128,256]{2,1,0:T(8,128)}) %reduce-scatter.26.cloned.1.call-update) | async-done | bytes 524304 | tf_op jit(solution)/shard_map/reduce_scatter | solution.py:187
  (246 shorter events, 83.8 us)
Async XLA Ops:
  7.2 64.2 %copy-start = (bf16[2048,256]{1,0:T(8,128)(2,1)S(1)}, bf16[2048,256]{1,0:T(8,128)(2,1)}, u32[]{:S(2)}) copy-start(bf16[2048,256]{1,0:T(8,128)(2,1)} %param.9) | copy-start | bytes 3145732
  7.2 58.7 %all-gather.6.cloned.1.call-start = ((), (), s32[]{:S(2)}) async-start(), calls=%async_computation.9 | async-start | bytes 1769472 | tf_op jit(solution)/shard_map/all_gather | solution.py:90
  8.9 93.2 %all-gather.8.cloned.1.call-start = ((), (), s32[]{:S(2)}) async-start(), calls=%async_computation.10 | async-start | bytes 1671168 | tf_op jit(solution)/shard_map/all_gather | solution.py:103
  69.8 68.0 %all-gather.10.cloned.1.call-start = ((), (), s32[]{:S(2)}) async-start(), calls=%async_computation.11 | async-start | bytes 1671168 | tf_op jit(solution)/shard_map/all_gather | solution.py:104
  70.9 146.8 %reduce-scatter.14.cloned.1.call-start = ((), (), s32[]{:S(2)}) async-start(), calls=%async_computation.12 | async-start | bytes 1769472 | tf_op jit(solution)/shard_map/reduce_scatter | solution.py:113
  71.4 33.3 %copy-start.12 = (pred[192,3072]{1,0:T(8,128)(4,1)}, pred[192,3072]{1,0:T(8,128)(4,1)S(1)}, u32[]{:S(2)}) copy-start(pred[192,3072]{1,0:T(8,128)(4,1)S(1)} %iota_compare_fusion) | copy-start | bytes 1769476
  71.8 35.7 %copy-start.46 = (bf16[24,2,8,128]{3,2,1,0:T(8,128)(2,1)}, bf16[24,2,8,128]{3,2,1,0:T(8,128)(2,1)S(1)}, u32[]{:S(2)}) copy-start(bf16[24,2,8,128]{3,2,1,0:T(8,128)(2,1)S(1)} %fusion.43) | copy-start | bytes 294916
  110.4 31.3 %copy-start.8 = (bf16[256,2048]{1,0:T(8,128)(2,1)S(1)}, bf16[256,2048]{1,0:T(8,128)(2,1)}, u32[]{:S(2)}) copy-start(bf16[256,2048]{1,0:T(8,128)(2,1)} %param.12) | copy-start | bytes 3145732
  141.7 76.0 %copy-start.57 = (bf16[192,256]{1,0:T(8,128)(2,1)S(1)}, bf16[192,256]{1,0:T(8,128)(2,1)}, u32[]{:S(2)}) copy-start(bf16[192,256]{1,0:T(8,128)(2,1)} %param.7) | copy-start | bytes 294916
  143.3 130.4 %copy-start.43 = (f32[2048]{0:T(1024)S(1)}, f32[2048]{0:T(1024)}, u32[]{:S(2)}) copy-start(f32[2048]{0:T(1024)} %param.8) | copy-start | bytes 24580
  143.3 128.6 %all-gather.12.cloned.1.call-start = ((), (), s32[]{:S(2)}) async-start(), calls=%async_computation.13 | async-start | bytes 1769472 | tf_op jit(solution)/shard_map/all_gather | solution.py:90
  219.4 135.0 %reduce-scatter.16.cloned.1.call-start = ((), (), s32[]{:S(2)}) async-start(), calls=%async_computation.14 | async-start | bytes 1769472 | tf_op jit(solution)/shard_map/reduce_scatter | solution.py:113
  273.8 383.8 %copy-start.66 = (f32[192]{0:T(256)}, f32[192]{0:T(256)S(1)}, u32[]{:S(2)}) copy-start(f32[192]{0:T(256)S(1)} %add_rsqrt_fusion.1) | copy-start | bytes 2308
  281.2 126.9 %all-gather.14.cloned.1.call-start = ((), (), s32[]{:S(2)}) async-start(), calls=%async_computation.15 | async-start | bytes 1769472 | tf_op jit(solution)/shard_map/all_gather | solution.py:90
  356.1 134.5 %reduce-scatter.18.cloned.1.call-start = ((), (), s32[]{:S(2)}) async-start(), calls=%async_computation.16 | async-start | bytes 1769472 | tf_op jit(solution)/shard_map/reduce_scatter | solution.py:113
  410.0 127.4 %copy-start.68 = (f32[192]{0:T(256)}, f32[192]{0:T(256)S(1)}, u32[]{:S(2)}) copy-start(f32[192]{0:T(256)S(1)} %add_rsqrt_fusion) | copy-start | bytes 2308
  417.4 194.8 %reduce-scatter.20.cloned.1.call-start = ((), (), s32[]{:S(2)}) async-start(), calls=%async_computation.17 | async-start | bytes 1769472 | tf_op jit(solution)/shard_map/reduce_scatter | solution.py:185
  490.6 40.0 %copy-start.15 = (bf16[3072,256]{0,1:T(8,128)(2,1)S(1)}, bf16[3072,256]{0,1:T(8,128)(2,1)}, u32[]{:S(2)}) copy-start(bf16[3072,256]{0,1:T(8,128)(2,1)} %copy.221) | copy-start | bytes 4718596
  539.0 193.5 %reduce-scatter.22.cloned.1.call-start = ((), (), s32[]{:S(2)}) async-start(), calls=%async_computation.18 | async-start | bytes 1769472 | tf_op jit(solution)/shard_map/reduce_scatter | solution.py:185
  612.3 37.8 %copy-start.11 = (bf16[256,2048]{1,0:T(8,128)(2,1)S(1)}, bf16[256,2048]{1,0:T(8,128)(2,1)}, u32[]{:S(2)}) copy-start(bf16[256,2048]{1,0:T(8,128)(2,1)} %param.12) | copy-start | bytes 3145732
  612.3 38.7 %copy-start.54 = (bf16[2,192,128]{2,1,0:T(8,128)(2,1)S(1)}, bf16[2,192,128]{2,1,0:T(8,128)(2,1)}, u32[]{:S(2)}) copy-start(bf16[2,192,128]{2,1,0:T(8,128)(2,1)} %copy-done.53) | copy-start | bytes 294916
  612.3 38.9 %copy-start.16 = (bf16[3072,256]{0,1:T(8,128)(2,1)S(1)}, bf16[3072,256]{0,1:T(8,128)(2,1)}, u32[]{:S(2)}) copy-start(bf16[3072,256]{0,1:T(8,128)(2,1)} %copy.221) | copy-start | bytes 4718596
  651.0 3.9 copy-start.34
  659.1 189.1 %reduce-scatter.28.cloned.1.call-start = ((), (), s32[]{:S(2)}) async-start(), calls=%async_computation.21 | async-start | bytes 3342336
  732.4 39.8 %copy-start.51 = (bf16[2,192,128]{2,1,0:T(8,128)(2,1)S(1)}, bf16[2,192,128]{2,1,0:T(8,128)(2,1)}, u32[]{:S(2)}) copy-start(bf16[2,192,128]{2,1,0:T(8,128)(2,1)} %copy-done.50) | copy-start | bytes 294916
  732.4 40.0 %copy-start.17 = (bf16[3072,256]{0,1:T(8,128)(2,1)S(1)}, bf16[3072,256]{0,1:T(8,128)(2,1)}, u32[]{:S(2)}) copy-start(bf16[3072,256]{0,1:T(8,128)(2,1)} %copy.221) | copy-start | bytes 4718596
  772.2 3.9 copy-start.36
  782.1 133.9 %reduce-scatter.30.cloned.1.call-start = ((), (), s32[]{:S(2)}) async-start(), calls=%async_computation.22 | async-start | bytes 3342336
  782.1 7.2 slice-start
  795.9 206.4 %reduce-scatter.24.cloned.1.call-start = ((), (), s32[]{:S(2)}) async-start(), calls=%async_computation.19 | async-start | bytes 1769472 | tf_op jit(solution)/shard_map/reduce_scatter | solution.py:185
  923.1 172.1 %reduce-scatter.26.cloned.1.call-start = ((), (), s32[]{:S(2)}) async-start(), calls=%async_computation.20 | async-start | bytes 8912896 | tf_op jit(solution)/shard_map/reduce_scatter | solution.py:187
  934.7 67.6 %copy-start.56 = (f32[192,256]{1,0:T(8,128)S(1)}, f32[192,256]{1,0:T(8,128)}, u32[]{:S(2)}) copy-start(f32[192,256]{1,0:T(8,128)} %get-tuple-element.31) | copy-start | bytes 589828
  (56 other events, 114.6 us)
Sparse Core Ops, SparseCore 0:
  10.8 55.0 all-gather.5
  69.9 32.1 all-gather.7
  104.4 33.3 all-gather.9
  143.4 74.2 reduce-scatter.13
  220.3 51.5 all-gather.11
  281.3 73.0 reduce-scatter.15
  356.6 51.5 all-gather.13
  417.5 73.0 reduce-scatter.17
  539.1 73.1 reduce-scatter.19
  659.2 73.1 reduce-scatter.21
  782.2 65.9 reduce-scatter.27
  850.5 65.4 reduce-scatter.29
  923.2 72.8 reduce-scatter.23
  998.3 96.8 reduce-scatter.25
where the time goes:
time: 1110 us; the launch traced here: 1100 us
  waiting for transfers between devices  781 us (70%)
  blocking collectives  174 us (16%)
  matrix products  73.4 us (7%)
  other arithmetic  30.4 us (3%)
  local copies, waits for them, and re-layouts  29.8 us (3%)
  between operations  15 us (1%)
    reduce_scatter x6, waiting for transfers between devices, body(): lax.psum_scatter(partial_value, 'head', scatter_dimension=1, tiled=True)  360 us
    all_gather x3, waiting for transfers between devices, body(): gathered = lax.all_gather(state, 'head', axis=1, tiled=True)  161 us
    unnamed x16, waiting for transfers between devices  111 us
    all_gather x3, blocking collectives, body(): grad_whole = lax.all_gather(grad_round, 'head', axis=1, tiled=True)  107 us
    reduce_scatter x1, waiting for transfers between devices, body(): summed = lax.psum_scatter(stacked, 'ctx', scatter_dimension=1, tiled=True)  91.2 us
    psum x1, blocking collectives, body(): grad_gain = lax.psum(grad_gain, ('ctx', 'head'))  66.9 us
    all_gather x1, waiting for transfers between devices, body(): lax.all_gather(own_keys, 'ctx', axis=0, tiled=True)  30.3 us
    all_gather x1, waiting for transfers between devices, body(): lax.all_gather(own_values, 'ctx', axis=0, tiled=True)  27.4 us
  transfers between devices with their start and end apart: 14, of which 13 were waited for; matrix products, arithmetic and copies ran while one was open for 4% of the time, Pallas kernels for 0%

commit v1 on v0

v1 whole, which is shorter than its diff:
```python
import math

import jax
import jax.numpy as jnp
from jax import lax
from jax.sharding import PartitionSpec as P

DH = 128
RECUR = 3

EPSILON = 1e-06
MASKED = -1e30
F32 = jnp.float32
BF16 = jnp.bfloat16


def dot(a, b):
    return jnp.dot(a, b, preferred_element_type=F32)


def dot_tn(a, b):
    return lax.dot_general(a, b, (((0,), (0,)), ((), ())), preferred_element_type=F32)


def dot_nt(a, b):
    return lax.dot_general(a, b, (((1,), (1,)), ((), ())), preferred_element_type=F32)


def inverse_of(state):
    return lax.rsqrt(jnp.mean(state * state, axis=-1, keepdims=True) + EPSILON)


def split_heads(block):
    return jnp.transpose(block.reshape(block.shape[0], -1, DH), (1, 0, 2))


def join_heads(block):
    return jnp.transpose(block, (1, 0, 2)).reshape(block.shape[1], -1)


def masked_scores(query, key_block, query_pos, key_pos):
    scaling = 1.0 / math.sqrt(query.shape[-1])
    scores = dot_nt(query, key_block) * scaling
    return jnp.where(key_pos[None, :] <= query_pos[:, None], scores, MASKED)


def attend(query, key_block, value_block, query_pos, key_pos):
    scores = masked_scores(query, key_block, query_pos, key_pos)
    row_max = jnp.max(scores, axis=-1, keepdims=True)
    weights = jnp.exp(scores - row_max)
    denominator = jnp.sum(weights, axis=-1, keepdims=True)
    probabilities = (weights / denominator).astype(BF16)
    attended = dot(probabilities, value_block).astype(BF16)
    return (attended, row_max[:, 0] + jnp.log(denominator[:, 0]))


def both_grads(query, key_block, value_block, grad_attended, row_dot, log_total, query_pos, key_pos):
    scaling = 1.0 / math.sqrt(query.shape[-1])
    scores = masked_scores(query, key_block, query_pos, key_pos)
    probabilities = jnp.exp(scores - log_total[:, None])
    grad_probs = dot_nt(grad_attended, value_block)
    grad_scores = (probabilities * (grad_probs - row_dot[:, None])).astype(BF16)
    grad_rows = (dot(grad_scores, key_block) * scaling).astype(BF16)
    key_term = dot_tn(grad_scores, query) * scaling
    value_term = dot_tn(probabilities.astype(BF16), grad_attended)
    return (grad_rows, key_term, value_term)


def body(tokens, norm_gain, w_query, w_key, w_value, w_out, teacher):
    rows, width = tokens.shape
    shards = lax.axis_size("ctx")
    heads = lax.axis_size("head")
    model = w_query.shape[0]
    chips = shards // 2
    ctx = lax.axis_index("ctx")
    head = lax.axis_index("head")
    core = ctx % 2
    same_core = [[2 * i + c for i in range(chips)] for c in range(2)]
    sibling = [(i, i ^ 1) for i in range(shards)]

    def gather_heads(x):
        return lax.all_to_all(jnp.broadcast_to(x[None], (heads,) + x.shape), "head", 0, 0)

    def whole_rows(x):
        got = gather_heads(x)
        return jnp.transpose(got, (1, 0, 2)).reshape(x.shape[0], -1)

    def swap(x):
        return lax.ppermute(x, "ctx", sibling)

    def gather_weight(w):
        half = w.shape[0] // 2
        mine = lax.all_gather(lax.dynamic_slice_in_dim(w, core * half, half, 0), "head", axis=0)
        mine = mine.reshape(heads * half, -1)
        return mine, swap(mine)

    def times_weight(x, weight):
        cut = x.reshape(rows, heads, 2, width // 2)
        here = lax.dynamic_index_in_dim(cut, core, 2, keepdims=False).reshape(rows, -1)
        there = lax.dynamic_index_in_dim(cut, 1 - core, 2, keepdims=False).reshape(rows, -1)
        return dot(here, weight[0]) + dot(there, weight[1])

    out_whole = gather_weight(w_out)
    teacher_whole = lax.all_gather(teacher, "head", axis=0)
    query_back = gather_weight(w_query.T)

    query_pos = ctx * rows + jnp.arange(rows, dtype=jnp.int32)
    chip_start = jnp.arange(chips, dtype=jnp.int32) * (2 * rows)
    block_start = jnp.concatenate([chip_start + core * rows, chip_start + (1 - core) * rows])
    key_pos = (block_start[:, None] + jnp.arange(rows, dtype=jnp.int32)[None, :]).reshape(-1)

    head_map = (0, 0, 0, None, None)
    grad_map = (0, 0, 0, 0, 0, 0, None, None)
    state = whole_rows(tokens).astype(F32)
    states, inverses, normed_list, queries, attended_list, totals = [state], [], [], [], [], []
    for level in range(RECUR):
        inverse = inverse_of(state)
        normed = (state * inverse * norm_gain).astype(BF16)
        query_rows = dot(normed, w_query).astype(BF16)
        if level == 0:
            own = jnp.concatenate([dot(normed, w_key).astype(BF16), dot(normed, w_value).astype(BF16)], 1)
            mine = lax.all_to_all(
                jnp.broadcast_to(own[None], (chips,) + own.shape), "ctx", 0, 0, axis_index_groups=same_core
            )
            both = jnp.concatenate([mine, swap(mine)], 0).reshape(shards * rows, 2 * width)
            key_heads = split_heads(both[:, :width])
            value_heads = split_heads(both[:, width:])
        attended_heads, log_total = jax.vmap(attend, in_axes=head_map)(
            split_heads(query_rows), key_heads, value_heads, query_pos, key_pos
        )
        attended = join_heads(attended_heads)
        state = state + times_weight(whole_rows(attended), out_whole)
        states.append(state)
        inverses.append(inverse)
        normed_list.append(normed)
        queries.append(query_rows)
        attended_list.append(attended)
        totals.append(log_total)

    weight = 1.0 / math.sqrt(rows * shards)
    own_columns = (jnp.arange(model, dtype=jnp.int32) // width == head).astype(F32)
    grad = jnp.zeros_like(state)
    gain_sum = jnp.zeros((model,), F32)
    key_sum = 0.0
    value_sum = 0.0
    grad_rounds, grad_queries = [], []
    for level in range(RECUR - 1, -1, -1):
        wanted = jnp.transpose(teacher_whole[:, level], (1, 0, 2)).reshape(rows, model)
        grad = grad + weight * (states[level + 1] - wanted.astype(F32))
        grad_round = grad.astype(BF16)
        grad_rounds.append(grad_round)
        grad_attended = dot_nt(grad_round, w_out).astype(BF16)
        grad_heads = split_heads(grad_attended)
        row_dot = jnp.sum(grad_heads.astype(F32) * split_heads(attended_list[level]).astype(F32), axis=-1)
        grad_query_heads, key_term, value_term = jax.vmap(both_grads, in_axes=grad_map)(
            split_heads(queries[level]),
            key_heads,
            value_heads,
            grad_heads,
            row_dot,
            totals[level],
            query_pos,
            key_pos,
        )
        key_sum = key_sum + key_term
        value_sum = value_sum + value_term
        grad_query_rows = join_heads(grad_query_heads)
        grad_queries.append(grad_query_rows)
        scaled = states[level] * inverses[level]
        if level > 0:
            grad_normed = times_weight(whole_rows(grad_query_rows), query_back)
        else:
            sums = jnp.concatenate([join_heads(key_sum), join_heads(value_sum)], 1).astype(BF16)
            sums = sums.reshape(2, chips, rows, 2 * width)
            pair = (sums[0].astype(F32) + swap(sums[1]).astype(F32)).astype(BF16)
            parts = lax.all_to_all(pair, "ctx", 0, 0, axis_index_groups=same_core)
            own_grads = jnp.sum(parts.astype(F32), axis=0).astype(BF16)
            grad_normed = dot_nt(grad_query_rows, w_query)
            grad_normed = grad_normed + dot_nt(own_grads[:, :width], w_key)
            grad_normed = grad_normed + dot_nt(own_grads[:, width:], w_value)
        gain_term = jnp.sum(grad_normed * scaled, axis=0)
        gain_sum = gain_sum + (gain_term * own_columns if level > 0 else gain_term)
        back = grad_normed * norm_gain
        step = inverses[level] * (back - scaled * jnp.mean(back * scaled, axis=-1, keepdims=True))
        if level > 0:
            grad = grad + step

    grad_query = dot_tn(
        jnp.concatenate([normed_list[2], normed_list[1], normed_list[0]], 0), jnp.concatenate(grad_queries, 0)
    )
    grad_out = dot_tn(
        jnp.concatenate(grad_rounds, 0),
        jnp.concatenate([attended_list[2], attended_list[1], attended_list[0]], 0),
    )
    grad_both = dot_tn(normed_list[0], own_grads)
    partial = jnp.concatenate([grad_query, grad_out, grad_both], 1).astype(BF16)
    slab = model // shards
    partial = partial.reshape(chips, 2, slab, 4 * width)
    gain_rows = gain_sum.reshape(-1, 4 * width).astype(BF16)
    gain_rows = jnp.broadcast_to(gain_rows[None], (chips,) + gain_rows.shape)
    here = lax.dynamic_index_in_dim(partial, core, 1, keepdims=False)
    there = lax.dynamic_index_in_dim(partial, 1 - core, 1, keepdims=False)
    here = jnp.concatenate([here, gain_rows], 1).astype(F32)
    there = swap(jnp.concatenate([there, gain_rows], 1)).astype(F32)
    parts = lax.all_to_all((here + there).astype(BF16), "ctx", 0, 0, axis_index_groups=same_core)
    summed = jnp.sum(parts.astype(F32), axis=0)
    gain_rows = summed[slab:].reshape(-1, width).astype(BF16)
    summed = summed[:slab]

    step = jnp.transpose(step.reshape(rows, heads, width), (1, 0, 2)).astype(BF16)
    gain_rows = jnp.broadcast_to(gain_rows[None], (heads,) + gain_rows.shape)
    parts = lax.all_to_all(jnp.concatenate([step, gain_rows], 1), "head", 0, 0)
    last = jnp.sum(parts.astype(F32), axis=0)
    grad_gain = last[rows:].reshape(-1)
    grad_input = lax.dynamic_slice_in_dim(grad, head * width, width, 1) + last[:rows]
    return (
        grad_input,
        grad_gain,
        summed[:, :width],
        summed[:, 2 * width : 3 * width],
        summed[:, 3 * width :],
        summed[:, width : 2 * width].T,
    )


def solution(mesh):
    return jax.shard_map(
        body,
        mesh=mesh,
        in_specs=(
            P("ctx", "head"),
            P(),
            P(None, "head"),
            P(None, "head"),
            P(None, "head"),
            P("head", None),
            P(None, "ctx", "head"),
        ),
        out_specs=(
            P("ctx", "head"),
            P(),
            P("ctx", "head"),
            P("ctx", "head"),
            P("ctx", "head"),
            P("head", "ctx"),
        ),
        check_vma=False,
    )
```

time: 1110 us -> 500 us (0.45)
  waiting for transfers between devices: 781 us -> 195 us
  blocking collectives: 174 us -> 35.7 us
  starting transfers between devices: 1.43 us -> 43.3 us
  local copies, waits for them, and re-layouts: 29.8 us -> 70.6 us
  matrix products: 73.4 us -> 97.1 us
    reduce_scatter x7 -> x0, waiting for transfers between devices: 451 us -> none  [the longest x6 360 us: body(): lax.psum_scatter(partial_value, 'head', scatter_dimension=1, tiled=True)]
    all_gather x5 -> x3, waiting for transfers between devices: 219 us -> 89.3 us  [the longest x2 89.3 us: gather_weight(): lax.all_gather(lax.dynamic_slice_in_dim(w, core * half, half, 0), 'head',...]
    unnamed x16 -> x3, waiting for transfers between devices: 111 us -> 0.73 us
    all_gather x3 -> x0, blocking collectives: 107 us -> none  [body(): grad_whole = lax.all_gather(grad_round, 'head', axis=1, tiled=True)]
    all_to_all x0 -> x9, waiting for transfers between devices: none -> 96.6 us  [the longest x6 50.4 us: gather_heads(): lax.all_to_all(jnp.broadcast_to(x[None], (heads,) + x.shape), 'head', 0, 0)]
    psum x1 -> x0, blocking collectives: 66.9 us -> none  [body(): grad_gain = lax.psum(grad_gain, ('ctx', 'head'))]
    all_to_all x0 -> x9, starting transfers between devices: none -> 42.7 us  [the longest x6 28.7 us: gather_heads(): lax.all_to_all(jnp.broadcast_to(x[None], (heads,) + x.shape), 'head', 0, 0)]
    all_to_all x0 -> x1, blocking collectives: none -> 35.7 us  [body(): lax.all_to_all(jnp.broadcast_to(own[None], (chips,) + own.shape), 'ctx',...]
  transfers between devices with their start and end apart: 14 -> 17, of which waited for: 13 -> 12; matrix products, arithmetic and copies ran while one was open for 4% -> 24% of each run, Pallas kernels for 0% -> 0%
where the time goes in v1:
time: 500 us; the launch traced here: 492 us
  waiting for transfers between devices  195 us (39%)
  matrix products  97.1 us (19%)
  local copies, waits for them, and re-layouts  70.6 us (14%)
  starting transfers between devices  43.3 us (9%)
  blocking collectives  35.7 us (7%)
  other arithmetic  34.9 us (7%)
  between operations  15.6 us (3%)
    all_gather x2, waiting for transfers between devices, gather_weight(): lax.all_gather(lax.dynamic_slice_in_dim(w, core * half, half, 0), 'head',...  89.3 us
    all_to_all x6, waiting for transfers between devices, gather_heads(): lax.all_to_all(jnp.broadcast_to(x[None], (heads,) + x.shape), 'head', 0, 0)  50.4 us
    dot_general x21, matrix products, dot(): return jnp.dot(a, b, preferred_element_type=F32)  47 us
    all_to_all x1, blocking collectives, body(): lax.all_to_all(jnp.broadcast_to(own[None], (chips,) + own.shape), 'ctx',...  35.7 us
    dot_general x9, matrix products, dot_tn(): lax.dot_general(a, b, (((0,), (0,)), ((), ())), preferred_element_type=F32)  32.3 us
    all_to_all x6, starting transfers between devices, gather_heads(): lax.all_to_all(jnp.broadcast_to(x[None], (heads,) + x.shape), 'head', 0, 0)  28.7 us
    unnamed x160, local copies, waits for them, and re-layouts  28.3 us
    all_to_all x1, waiting for transfers between devices, body(): lax.all_to_all((here + there).astype(BF16), 'ctx', 0, 0, axis_index_group...  27.2 us
  transfers between devices with their start and end apart: 17, of which 12 were waited for; matrix products, arithmetic and copies ran while one was open for 24% of the time, Pallas kernels for 0%

profile of v1, /device:TPU:0, one launch (start us, length us, event | category | flops | bytes accessed | tf_op | source)
XLA Modules:
  0.0 491.9 jit_solution(7612997809018495721)
XLA Ops:
  11.1 7.0 %all-to-all-start = ((bf16[8,192,256]{2,1,0:T(8,128)(2,1)}), bf16[8,192,256]{2,1,0:T(8,128)(2,1)S(1)}, u32[]{:S(2)}, u32[]{:S(2)}) async-start(bf16[8,192,256]{2,1,0:T(8,128)(2,1)} %broadcast_in_dim.46), calls=%async_computation | async-start | bytes 1572864 | tf_op jit(solution)/shard_map/all_to_all | solution.py:82
  19.0 15.1 %all-to-all-done = bf16[8,192,256]{2,1,0:T(8,128)(2,1)S(1)} async-done(((bf16[8,192,256]{2,1,0:T(8,128)(2,1)}), bf16[8,192,256]{2,1,0:T(8,128)(2,1)S(1)}, u32[]{:S(2)}, u32[]{:S(2)}) %all-to-all-start) | async-done | bytes 786464 | tf_op jit(solution)/shard_map/all_to_all | solution.py:82
  37.1 35.7 %all_to_all.50 = bf16[8,192,512]{2,1,0:T(8,128)(2,1)S(1)} all-to-all(bf16[8,192,512]{2,1,0:T(8,128)(2,1)S(1)} %broadcast_in_dim.48), channel_id=1, replica_groups={{0,16,32,48,64,80,96,112},{8,24,40,56,72,88,104,120},{1,17,33,49,65,81,..., dimensions={0} | all-to-all | bytes 3145728 | tf_op jit(solution)/shard_map/all_to_all | solution.py:122
  74.0 20.2 %all-gather.7.cloned.1.call-done = bf16[1024,2048]{1,0:T(8,128)(2,1)} async-done(((bf16[128,2048]{1,0:T(8,128)(2,1)}), bf16[1024,2048]{1,0:T(8,128)(2,1)}) %all-gather.7.cloned.1.call-update) | async-done | bytes 4194320 | tf_op jit(solution)/shard_map/all_gather | solution.py:93
  115.4 4.4 all-to-all-start.2
  119.9 17.3 %all-to-all-done.2 = bf16[8,192,256]{2,1,0:T(8,128)(2,1)} async-done(((bf16[8,192,256]{2,1,0:T(8,128)(2,1)}), bf16[8,192,256]{2,1,0:T(8,128)(2,1)}, u32[]{:S(2)}, u32[]{:S(2)}) %all-to-all-start.2) | async-done | bytes 786464 | tf_op jit(solution)/shard_map/all_to_all | solution.py:82
  154.7 4.2 all-to-all-start.3
  166.2 69.2 %all-gather.11.cloned.1.call-done = bf16[1024,2048]{0,1:T(8,128)(2,1)} async-done(((bf16[128,2048]{0,1:T(8,128)(2,1)}), bf16[1024,2048]{0,1:T(8,128)(2,1)}) %all-gather.11.cloned.1.call-update) | async-done | bytes 4194320 | tf_op jit(solution)/shard_map/all_gather | solution.py:93
  253.2 4.2 all-to-all-start.4
  260.8 10.8 %all-to-all-done.4 = bf16[8,192,256]{2,1,0:T(8,128)(2,1)} async-done(((bf16[8,192,256]{2,1,0:T(8,128)(2,1)}), bf16[8,192,256]{2,1,0:T(8,128)(2,1)}, u32[]{:S(2)}, u32[]{:S(2)}) %all-to-all-start.4) | async-done | bytes 786464 | tf_op jit(solution)/shard_map/all_to_all | solution.py:82
  276.7 4.7 fusion.161
  288.0 4.4 all-to-all-start.5
  292.4 4.0 fusion.134
  296.4 5.1 %fusion.17 = f32[2,3072,128]{1,2,0:T(8,128)} fusion(f32[2,192,3072]{2,1,0:T(8,128)} %copy-done.2, f32[2,192]{1,0:T(2,128)S(1)} %log_add_fusion.2, bf16[24,2,8,128]{3,2,1,0:T(8,128)(2,1)S(1)} %fusion.82), kind=kOutput, calls=%fused_computation.52 | convolution fusion | flops 304349184 | bytes 7964160 | tf_op jit(solution)/shard_map/vmap()/dot_general | solution.py:22
  301.4 4.3 all-to-all-done.5
  307.4 3.8 fusion.105
  311.3 4.2 multiply_reduce_fusion.2
  324.7 4.4 all-to-all-start.6
  329.1 5.2 %convolution_add_fusion.3 = f32[2,3072,128]{1,2,0:T(8,128)} fusion(f32[2,3072,128]{1,2,0:T(8,128)} %fusion.134, bf16[2,192,3072]{2,1,0:T(8,128)(2,1)} %copy-done.19, bf16[24,2,8,128]{3,2,1,0:T(8,128)(2,1)} %copy-done.52), kind=kOutput, calls=%fused_computation.27 | convolution fusion | flops 302776320 | bytes 8749056 | tf_op jit(solution)/shard_map/vmap()/dot_general | solution.py:22
  334.3 5.3 %convolution_add_fusion.1 = f32[2,3072,128]{1,2,0:T(8,128)} fusion(f32[2,3072,128]{1,2,0:T(8,128)S(1)} %copy-done.24, f32[2,192,3072]{2,1,0:T(8,128)} %copy-done.1, f32[2,192]{1,0:T(2,128)S(1)} %log_add_fusion.1, bf16[24,2,8,128]{3,2,1,0:T(8,128)(2,1)S(1)} %fusion.83), kind=kOutput, calls=%fused_computation.25 | convolution fusion | flops 305135616 | bytes 11109888 | tf_op jit(solution)/shard_map/vmap()/dot_general | solution.py:22
  344.0 3.8 fusion.100
  347.8 4.2 multiply_reduce_fusion.1
  363.9 4.4 fusion.7
  370.9 3.8 pad_maximum_fusion.4
  374.7 3.7 collective-permute-done.3
  382.0 4.7 all-to-all-start.7
  401.1 7.3 %all-to-all-done.7 = bf16[8,192,512]{2,1,0:T(8,128)(2,1)} async-done(((bf16[8,192,512]{2,1,0:T(8,128)(2,1)}), bf16[8,192,512]{2,1,0:T(8,128)(2,1)}, u32[]{:S(2)}, u32[]{:S(2)}) %all-to-all-start.7) | async-done | bytes 1572896 | tf_op jit(solution)/shard_map/all_to_all | solution.py:176
  420.8 4.2 collective-permute-done.4
  427.9 4.4 all-to-all-start.8
  434.1 27.2 %all-to-all-done.8 = bf16[8,130,1024]{2,1,0:T(8,128)(2,1)} async-done(((bf16[8,130,1024]{2,1,0:T(8,128)(2,1)}), bf16[8,130,1024]{2,1,0:T(8,128)(2,1)}, u32[]{:S(2)}, u32[]{:S(2)}) %all-to-all-start.8) | async-done | bytes 2129952 | tf_op jit(solution)/shard_map/all_to_all | solution.py:205
  464.4 4.9 all-to-all-start.9
  470.8 11.7 %all-to-all-done.9 = bf16[8,200,256]{2,1,0:T(8,128)(2,1)S(1)} async-done(((bf16[8,200,256]{2,1,0:T(8,128)(2,1)}), bf16[8,200,256]{2,1,0:T(8,128)(2,1)S(1)}, u32[]{:S(2)}, u32[]{:S(2)}) %all-to-all-start.9) | async-done | bytes 819232 | tf_op jit(solution)/shard_map/all_to_all | solution.py:212
  (303 shorter events, 158.4 us)
Async XLA Ops:
  7.2 65.7 %copy-start = (bf16[2048,256]{1,0:T(8,128)(2,1)S(1)}, bf16[2048,256]{1,0:T(8,128)(2,1)}, u32[]{:S(2)}) copy-start(bf16[2048,256]{1,0:T(8,128)(2,1)} %param.9) | copy-start | bytes 3145732
  7.2 87.0 %all-gather.7.cloned.1.call-start = ((), (), s32[]{:S(2)}) async-start(), calls=%async_computation.10 | async-start | bytes 4718592 | tf_op jit(solution)/shard_map/all_gather | solution.py:93
  11.1 22.9 %all-to-all-start = ((bf16[8,192,256]{2,1,0:T(8,128)(2,1)}), bf16[8,192,256]{2,1,0:T(8,128)(2,1)S(1)}, u32[]{:S(2)}, u32[]{:S(2)}) async-start(bf16[8,192,256]{2,1,0:T(8,128)(2,1)} %broadcast_in_dim.46), calls=%async_computation | async-start | bytes 1572864 | tf_op jit(solution)/shard_map/all_to_all | solution.py:82
  18.2 140.8 %all-gather.9.cloned.1.call-start = ((), (), s32[]{:S(2)}) async-start(), calls=%async_computation.11 | async-start | bytes 2654208 | tf_op jit(solution)/shard_map/all_gather | solution.py:104
  18.9 216.4 %all-gather.11.cloned.1.call-start = ((), (), s32[]{:S(2)}) async-start(), calls=%async_computation.12 | async-start | bytes 4718592 | tf_op jit(solution)/shard_map/all_gather | solution.py:93
  72.9 22.9 %collective-permute-start = (bf16[8,192,512]{2,1,0:T(8,128)(2,1)S(1)}, bf16[8,192,512]{2,1,0:T(8,128)(2,1)}, u32[]{:S(2)}, u32[]{:S(2)}) collective-permute-start(bf16[8,192,512]{2,1,0:T(8,128)(2,1)S(1)} %all_to_all.50), channel_id=1, source_target_pairs={{0,8},{8,0},{16,24},{24,16},{32,40},{40,32},{48,56},{56,48},{64,72... | collective-permute-start | bytes 4718600 | tf_op jit(solution)/shard_map/ppermute | solution.py:89
  94.1 48.0 %collective-permute-start.1 = (bf16[1024,2048]{1,0:T(8,128)(2,1)}, bf16[1024,2048]{1,0:T(8,128)(2,1)}, u32[]{:S(2)}, u32[]{:S(2)}) collective-permute-start(bf16[1024,2048]{1,0:T(8,128)(2,1)} %all-gather.7.cloned.1.call-done), channel_id=1, source_target_pairs={{0,8},{8,0},{16,24},{24,16},{32,40},{40,32},{48,56},{56,48},{64,72... | collective-permute-start | bytes 12582920 | tf_op jit(solution)/shard_map/ppermute | solution.py:89
  95.7 12.1 %copy-start.50 = (bf16[24,2,8,128]{3,2,1,0:T(8,128)(2,1)}, bf16[24,2,8,128]{3,2,1,0:T(8,128)(2,1)S(1)}, u32[]{:S(2)}) copy-start(bf16[24,2,8,128]{3,2,1,0:T(8,128)(2,1)S(1)} %fusion.79) | copy-start | bytes 294916
  114.4 24.4 %copy-start.55 = (bf16[192,256]{1,0:T(8,128)(2,1)}, bf16[192,256]{1,0:T(8,128)(2,1)S(1)}, u32[]{:S(2)}) copy-start(bf16[192,256]{1,0:T(8,128)(2,1)S(1)} %copy_bitcast_fusion.13) | copy-start | bytes 294916
  115.4 21.8 %all-to-all-start.2 = ((bf16[8,192,256]{2,1,0:T(8,128)(2,1)}), bf16[8,192,256]{2,1,0:T(8,128)(2,1)}, u32[]{:S(2)}, u32[]{:S(2)}) async-start(bf16[8,192,256]{2,1,0:T(8,128)(2,1)} %broadcast_in_dim.51), calls=%async_computation.2 | async-start | bytes 1572864 | tf_op jit(solution)/shard_map/all_to_all | solution.py:82
  153.7 8.0 %copy-start.57 = (bf16[192,256]{1,0:T(8,128)(2,1)}, bf16[192,256]{1,0:T(8,128)(2,1)S(1)}, u32[]{:S(2)}) copy-start(bf16[192,256]{1,0:T(8,128)(2,1)S(1)} %copy_bitcast_fusion.12) | copy-start | bytes 294916
  154.7 81.0 %all-to-all-start.3 = ((bf16[8,192,256]{2,1,0:T(8,128)(2,1)}), bf16[8,192,256]{2,1,0:T(8,128)(2,1)}, u32[]{:S(2)}, u32[]{:S(2)}) async-start(bf16[8,192,256]{2,1,0:T(8,128)(2,1)} %broadcast_in_dim.53), calls=%async_computation.3 | async-start | bytes 1572864 | tf_op jit(solution)/shard_map/all_to_all | solution.py:82
  235.3 75.9 %collective-permute-start.2 = (bf16[1024,2048]{0,1:T(8,128)(2,1)}, bf16[1024,2048]{0,1:T(8,128)(2,1)}, u32[]{:S(2)}, u32[]{:S(2)}) collective-permute-start(bf16[1024,2048]{0,1:T(8,128)(2,1)} %all-gather.11.cloned.1.call-done), channel_id=1, source_target_pairs={{0,8},{8,0},{16,24},{24,16},{32,40},{40,32},{48,56},{56,48},{64,72... | collective-permute-start | bytes 12582920 | tf_op jit(solution)/shard_map/ppermute | solution.py:89
  252.2 6.8 %copy-start.61 = (bf16[192,256]{1,0:T(8,128)(2,1)}, bf16[192,256]{1,0:T(8,128)(2,1)S(1)}, u32[]{:S(2)}) copy-start(bf16[192,256]{1,0:T(8,128)(2,1)S(1)} %copy_bitcast_fusion.11) | copy-start | bytes 294916
  253.2 18.4 %all-to-all-start.4 = ((bf16[8,192,256]{2,1,0:T(8,128)(2,1)}), bf16[8,192,256]{2,1,0:T(8,128)(2,1)}, u32[]{:S(2)}, u32[]{:S(2)}) async-start(bf16[8,192,256]{2,1,0:T(8,128)(2,1)} %broadcast_in_dim.55), calls=%async_computation.4 | async-start | bytes 1572864 | tf_op jit(solution)/shard_map/all_to_all | solution.py:82
  276.6 5.8 %slice-start.2 = ((s8[4718592]{0:T(1024)(128)(4,1)}), s8[4194304]{0:T(1024)(128)(4,1)S(1)}, s32[]{:S(2)}) async-start(s8[4718592]{0:T(1024)(128)(4,1)} %bitcast.379), calls=%async_computation.15 | async-start | bytes 8388608
  276.6 4.7 copy-start.21
  276.6 5.6 %copy-start.70 = (bf16[2,192,128]{2,1,0:T(8,128)(2,1)S(1)}, bf16[2,192,128]{2,1,0:T(8,128)(2,1)}, u32[]{:S(2)}) copy-start(bf16[2,192,128]{2,1,0:T(8,128)(2,1)} %copy-done.69) | copy-start | bytes 294916
  276.7 5.8 %slice-start.3 = ((s8[4718592]{0:T(1024)(128)(4,1)}), s8[524288]{0:T(1024)(128)(4,1)S(1)}, s32[]{:S(2)}) async-start(s8[4718592]{0:T(1024)(128)(4,1)} %bitcast.379), calls=%async_computation.16 | async-start | bytes 1048576
  288.0 17.8 %all-to-all-start.5 = ((bf16[8,192,256]{2,1,0:T(8,128)(2,1)}), bf16[8,192,256]{2,1,0:T(8,128)(2,1)}, u32[]{:S(2)}, u32[]{:S(2)}) async-start(bf16[8,192,256]{2,1,0:T(8,128)(2,1)} %broadcast_in_dim.57), calls=%async_computation.5 | async-start | bytes 1572864 | tf_op jit(solution)/shard_map/all_to_all | solution.py:82
  311.3 4.2 copy-start.29
  311.3 4.2 copy-start.32
  324.7 17.6 %all-to-all-start.6 = ((bf16[8,192,256]{2,1,0:T(8,128)(2,1)}), bf16[8,192,256]{2,1,0:T(8,128)(2,1)}, u32[]{:S(2)}, u32[]{:S(2)}) async-start(bf16[8,192,256]{2,1,0:T(8,128)(2,1)} %broadcast_in_dim.59), calls=%async_computation.6 | async-start | bytes 1572864 | tf_op jit(solution)/shard_map/all_to_all | solution.py:82
  329.1 5.2 %copy-start.24 = (f32[2,3072,128]{1,2,0:T(8,128)S(1)}, f32[2,3072,128]{1,2,0:T(8,128)}, u32[]{:S(2)}) copy-start(f32[2,3072,128]{1,2,0:T(8,128)} %fusion.17) | copy-start | bytes 9437188
  347.8 4.2 copy-start.28
  347.8 4.2 copy-start.31
  354.0 4.9 copy-start.45
  374.7 3.8 collective-permute-start.3
  382.0 26.5 %all-to-all-start.7 = ((bf16[8,192,512]{2,1,0:T(8,128)(2,1)}), bf16[8,192,512]{2,1,0:T(8,128)(2,1)}, u32[]{:S(2)}, u32[]{:S(2)}) async-start(bf16[8,192,512]{2,1,0:T(8,128)(2,1)} %fusion.9), calls=%async_computation.7 | async-start | bytes 3145728 | tf_op jit(solution)/shard_map/all_to_all | solution.py:176
  420.7 4.3 collective-permute-start.4
  427.9 33.4 %all-to-all-start.8 = ((bf16[8,130,1024]{2,1,0:T(8,128)(2,1)}), bf16[8,130,1024]{2,1,0:T(8,128)(2,1)}, u32[]{:S(2)}, u32[]{:S(2)}) async-start(bf16[8,130,1024]{2,1,0:T(8,128)(2,1)} %add_convert_fusion), calls=%async_computation.8 | async-start | bytes 4456448 | tf_op jit(solution)/shard_map/all_to_all | solution.py:205
  464.4 18.1 %all-to-all-start.9 = ((bf16[8,200,256]{2,1,0:T(8,128)(2,1)}), bf16[8,200,256]{2,1,0:T(8,128)(2,1)S(1)}, u32[]{:S(2)}, u32[]{:S(2)}) async-start(bf16[8,200,256]{2,1,0:T(8,128)(2,1)} %pad_maximum_fusion.5), calls=%async_computation.9 | async-start | bytes 1638400 | tf_op jit(solution)/shard_map/all_to_all | solution.py:212
  (62 other events, 134.3 us)
Sparse Core Ops, SparseCore 0:
  10.3 83.7 all-gather.6
  96.5 57.8 all-gather.8
  156.6 78.7 all-gather.10
